TPU v7x, 32 devices: a whole 2x2x4 slice. The times are simulated.
32 devices in a mesh: sub: 8 (over y, x, core), rep: 4 (over z).
Axes of the slice: x: 2, y: 2, z: 4, core: 2. Of those that a mesh axis runs over, the one named last changes fastest.
Arguments:
- rhs: float32 [2048, 128], P('sub'), may hold values from -31 to 31
- schur_diag: bfloat16 [2048, 256], P('sub'), may hold values from -0.375 to 0.375
- precond: bfloat16 [2048, 512], P('sub'), may hold values from -0.25 to 0.25
- halo_ids: int32 [8, 2], P('sub'), may hold values from 0 to 15, as said below
- factors: bfloat16 [64, 1024, 1024], P(('sub', 'rep')), may hold values from -0.1875 to 0.1875
- couplings: bfloat16 [64, 1024, 512], P(('sub', 'rep')), may hold values from -0.09375 to 0.09375
- block_ids: int32 [64, 4], P(('sub', 'rep')), may hold values from 0 to 15
- counts: int32 [32], P(('sub', 'rep')), may hold values from 1 to 2, 40 in all
Outputs:
- solution: float32 [2048, 128], P('sub')
Inputs may be any that keep to these rules, and one draw needn't show every extreme that they name: `halo_ids`: in row d the first 1 entries name blocks owned by index d - 1 of sub and the others blocks owned by index d + 1, cyclically; block b is owned by index b // 2. counts[i] belongs to device i of sub+rep, sub slowest; slots k with k % 2 >= counts[k // 2] are not part of the operator.
All inputs are finite; a program needn't handle non-finite values.
Results may differ from a plain program's by a relative error of at most 0.0031.
Values may be sent and summed in bfloat16 or wider, within the bound.
A program may use at most 64 MiB of HBM per device.

v0:
```python
import jax
import jax.numpy as jnp
from jax import lax
from jax.sharding import PartitionSpec as P

BI = 128
GB_DEV = 2


def padded_2(cells, sides, width):
    for axis, dim in sides:
        count = lax.axis_size(axis)
        head = lax.slice_in_dim(cells, 0, width, axis=dim)
        tail = lax.slice_in_dim(cells, cells.shape[dim] - width, cells.shape[dim], axis=dim)
        cells = jnp.concatenate(
            [
                lax.ppermute(tail, axis, [(i, (i + 1) % count) for i in range(count)]),
                cells,
                lax.ppermute(head, axis, [((i + 1) % count, i) for i in range(count)]),
            ],
            axis=dim,
        )
    return cells


def column_sums(left, right):
    return jnp.sum(left * right, axis=0)


def on_device(rhs, schur_diag, precond, halo_ids, factors, couplings, block_ids, counts):
    rows_here = rhs.shape[0]
    columns = rhs.shape[1]
    sub_count = lax.axis_size("sub")
    transposed = (((0,), (0,)), ((), ()))

    def apply_schur(field):
        rounded = field.astype(jnp.bfloat16)
        whole = lax.all_gather(rounded, "sub", axis=0, tiled=True)
        blocks = whole.reshape(-1, BI, columns)
        width = block_ids.shape[1] * BI

        def slot_step(slot, total):
            listed = block_ids[slot]
            picked = blocks[listed].reshape(width, columns)
            factor = factors[slot]
            coupling = couplings[slot]
            first = jnp.dot(coupling, picked, preferred_element_type=jnp.float32).astype(
                jnp.bfloat16
            )
            second = jnp.dot(factor, first, preferred_element_type=jnp.float32).astype(jnp.bfloat16)
            third = lax.dot_general(
                factor, second, transposed, preferred_element_type=jnp.float32
            ).astype(jnp.bfloat16)
            fourth = lax.dot_general(
                coupling, third, transposed, preferred_element_type=jnp.float32
            )
            return total.at[listed].add(fourth.reshape(-1, BI, columns))

        total = lax.fori_loop(0, counts[0], slot_step, jnp.zeros(blocks.shape, jnp.float32))
        flat = total.reshape(-1, columns)
        coupled = lax.psum_scatter(lax.psum(flat, "rep"), "sub", scatter_dimension=0, tiled=True)
        local = jnp.dot(schur_diag, rounded, preferred_element_type=jnp.float32)
        return 3.0 * field + local - coupled

    def precondition(field):
        listed = halo_ids[0]
        rounded = field.astype(jnp.bfloat16)
        padded = padded_2(rounded, (("sub", 0),), rows_here)
        owner = listed // GB_DEV
        place = (owner - lax.axis_index("sub") + 1) % sub_count * GB_DEV + listed % GB_DEV
        halo_rows = padded.reshape(-1, BI, columns)[place]
        extended = jnp.concatenate([rounded, halo_rows.reshape(-1, columns)], axis=0)
        return field + jnp.dot(precond, extended, preferred_element_type=jnp.float32)

    def orthogonal(field, basis):
        stacked = jnp.stack(basis)
        local_sums = jnp.concatenate(
            [jnp.sum(stacked * field[None], axis=1), column_sums(field, field)[None]], axis=0
        )
        totals = lax.psum(local_sums, "sub")
        coeffs = totals[:-1]
        rest = field - jnp.sum(coeffs[:, None, :] * stacked, axis=0)
        length = jnp.sqrt(totals[-1] - jnp.sum(coeffs * coeffs, axis=0))
        return (coeffs, rest, length)

    start_norm = jnp.sqrt(lax.psum(column_sums(rhs, rhs), "sub"))
    first_basis = rhs / start_norm
    first_dir = precondition(first_basis)
    coeffs_one, rest_one, length_one = orthogonal(apply_schur(first_dir), [first_basis])
    second_basis = rest_one / length_one
    second_dir = precondition(second_basis)
    coeffs_two, rest_two, length_two = orthogonal(
        apply_schur(second_dir), [first_basis, second_basis]
    )
    upper_one = coeffs_one[0]
    upper_two = coeffs_two[0]
    middle = coeffs_two[1]
    radius_one = jnp.sqrt(upper_one * upper_one + length_one * length_one)
    cosine_one = upper_one / radius_one
    sine_one = length_one / radius_one
    rotated_top = cosine_one * upper_two + sine_one * middle
    rotated_low = cosine_one * middle - sine_one * upper_two
    weight_two = (
        -rotated_low * sine_one * start_norm / (rotated_low * rotated_low + length_two * length_two)
    )
    weight_one = (cosine_one * start_norm - rotated_top * weight_two) / radius_one
    return weight_one * first_dir + weight_two * second_dir


def solution(mesh):
    placed = (
        P("sub", None),
        P("sub", None),
        P("sub", None),
        P("sub", None),
        P(("sub", "rep"), None, None),
        P(("sub", "rep"), None, None),
        P(("sub", "rep"), None),
        P(("sub", "rep")),
    )
    return jax.shard_map(
        on_device, mesh=mesh, in_specs=placed, out_specs=P("sub", None), check_vma=False
    )
```

profile of v0, /device:TPU:0, one launch (start us, length us, event | category | flops | bytes accessed | tf_op | source)
XLA Modules:
  0.0 301.9 jit_solution(1615976823002647912)
XLA Ops:
  8.6 15.1 %psum.35 = f32[128]{0:T(128)S(1)} all-reduce(f32[128]{0:T(128)S(1)} %multiply_reduce_fusion.3), channel_id=1, replica_groups=mesh['sub'=8,'rep'=4] {'sub'}, use_global_device_ids=true, to_apply=%region_1.0 | all-reduce | flops 128 | bytes 1024 | tf_op jit(solution)/shard_map/psum | solution.py:86
  24.4 3.0 copy.20
  30.9 9.9 %all_gather.6 = bf16[2048,128]{0,1:T(8,128)(2,1)S(1)} all-gather(bf16[256,128]{0,1:T(8,128)(2,1)S(1)} %get-tuple-element.148), channel_id=1, replica_groups=mesh['sub'=8,'rep'=4] {'sub'}, dimensions={0}, use_global_device_ids=true | all-gather | bytes 589824 | tf_op jit(solution)/shard_map/all_gather | solution.py:38
  42.9 13.7 %while.20 = (s32[]{:T(128)}, f32[16,128,128]{2,1,0:T(8,128)}, s32[]{:T(128)}, s32[2,4]{1,0:T(2,128)}, bf16[2,1024,512]{1,2,0:T(8,128)(2,1)S(1)}, /*index=5*/bf16...) while((s32[]{:T(128)}, f32[16,128,128]{2,1,0:T(8,128)}, ...), condition=%wide.region_4.5_spmd, body=%wide.region_2.4_spmd.sunk | while | flops 805766144 | bytes 10360043 | solution.py:59
  44.4 1.6 gather_fusion
  46.0 3.8 %fusion.120 = bf16[1024,128]{1,0:T(8,128)(2,1)} fusion(bf16[2,1024,1024]{2,1,0:T(8,128)(2,1)} %get-tuple-element.267, s32[]{:T(128)S(6)} %select_n.120, bf16[512,128]{1,0:T(8,128)(2,1)S(1)} %bitcast.236, bf16[2,1024,512]{1,2,0:T(8,128)(2,1)S(1)} %get-tuple-element.266), kind=kOutput, calls=%fused_computation.12.clone.1 | convolution fusion | flops 402915328 | bytes 3539968 | tf_op jit(solution)/shard_map/while/body/dot_general | solution.py:50
  49.8 3.7 %fusion.121 = f32[4,128,128]{2,1,0:T(8,128)} fusion(bf16[4,128,1024]{2,1,0:T(8,128)(2,1)S(1)} %bitcast.232, bf16[1024,128]{1,0:T(8,128)(2,1)} %fusion.120, bf16[2,1024,1024]{2,1,0:T(8,128)(2,1)} %get-tuple-element.267, s32[]{:T(128)S(6)} %select_n.120), kind=kOutput, calls=%fused_computation.17.clone.1 | convolution fusion | flops 402784256 | bytes 3670020 | tf_op jit(solution)/shard_map/while/body/dot_general | solution.py:54
  53.5 2.5 scatter_fusion
  56.7 2.6 copy.31
  59.4 49.5 %reduce-scatter.3.cloned.1.call-done = f32[256,128]{0,1:T(8,128)} async-done(((f32[2048,128]{0,1:T(8,128)}), f32[256,128]{0,1:T(8,128)}) %reduce-scatter.3.cloned.1.call-update) | async-done | bytes 131088 | tf_op jit(solution)/shard_map/reduce_scatter | solution.py:61
  109.0 36.6 %all-reduce.3.cloned.1.call-done = f32[256,128]{0,1:T(8,128)} async-done(((f32[256,128]{0,1:T(8,128)}), f32[256,128]{0,1:T(8,128)}) %all-reduce.3.cloned.1.call-update) | async-done | bytes 131088 | tf_op jit(solution)/shard_map/psum | solution.py:61
  147.6 11.8 %psum.37 = f32[2,128]{1,0:T(2,128)S(1)} all-reduce(f32[2,128]{1,0:T(2,128)S(1)} %pad_maximum_fusion.3), channel_id=1, replica_groups=mesh['sub'=8,'rep'=4] {'sub'}, use_global_device_ids=true, to_apply=%region_9.10 | all-reduce | flops 256 | bytes 2048 | tf_op jit(solution)/shard_map/psum | solution.py:80
  160.7 1.4 collective-permute-done.3
  162.2 3.4 %collective-permute-done.2 = bf16[256,128]{0,1:T(8,128)(2,1)S(1)} collective-permute-done((bf16[256,128]{0,1:T(8,128)(2,1)S(1)}, bf16[256,128]{0,1:T(8,128)(2,1)S(1)}, u32[]{:S(2)}, u32[]{:S(2)}) %collective-permute-start.2) | collective-permute-done | bytes 65568 | tf_op jit(solution)/shard_map/ppermute | solution.py:17
  167.9 10.2 %all_gather.7 = bf16[2048,128]{0,1:T(8,128)(2,1)S(1)} all-gather(bf16[256,128]{0,1:T(8,128)(2,1)S(1)} %get-tuple-element.150), channel_id=1, replica_groups=mesh['sub'=8,'rep'=4] {'sub'}, dimensions={0}, use_global_device_ids=true | all-gather | bytes 589824 | tf_op jit(solution)/shard_map/all_gather | solution.py:38
  180.2 13.7 %while.21 = (s32[]{:T(128)}, f32[16,128,128]{2,1,0:T(8,128)}, s32[]{:T(128)}, s32[2,4]{1,0:T(2,128)}, bf16[2,1024,512]{1,2,0:T(8,128)(2,1)S(1)}, /*index=5*/bf16...) while((s32[]{:T(128)}, f32[16,128,128]{2,1,0:T(8,128)}, ...), condition=%wide.region_12.13_spmd, body=%wide.region_10.12_spmd.sunk | while | flops 805766144 | bytes 10360043 | solution.py:59
  181.6 1.6 gather_fusion.1
  183.3 3.8 %fusion.129 = bf16[1024,128]{1,0:T(8,128)(2,1)} fusion(bf16[2,1024,1024]{2,1,0:T(8,128)(2,1)} %get-tuple-element.297, s32[]{:T(128)S(6)} %select_n.122, bf16[512,128]{1,0:T(8,128)(2,1)S(1)} %bitcast.237, bf16[2,1024,512]{1,2,0:T(8,128)(2,1)S(1)} %get-tuple-element.296), kind=kOutput, calls=%fused_computation.32.clone.1 | convolution fusion | flops 402915328 | bytes 3539968 | tf_op jit(solution)/shard_map/while/body/dot_general | solution.py:50
  187.1 3.7 %fusion.130 = f32[4,128,128]{2,1,0:T(8,128)} fusion(bf16[4,128,1024]{2,1,0:T(8,128)(2,1)S(1)} %bitcast.233, bf16[1024,128]{1,0:T(8,128)(2,1)} %fusion.129, bf16[2,1024,1024]{2,1,0:T(8,128)(2,1)} %get-tuple-element.297, s32[]{:T(128)S(6)} %select_n.122), kind=kOutput, calls=%fused_computation.37.clone.1 | convolution fusion | flops 402784256 | bytes 3670020 | tf_op jit(solution)/shard_map/while/body/dot_general | solution.py:54
  190.8 2.5 scatter_fusion.1
  194.0 2.7 copy.34
  196.8 47.8 %reduce-scatter.5.cloned.1.call-done = f32[256,128]{0,1:T(8,128)} async-done(((f32[2048,128]{0,1:T(8,128)}), f32[256,128]{0,1:T(8,128)}) %reduce-scatter.5.cloned.1.call-update) | async-done | bytes 131088 | tf_op jit(solution)/shard_map/reduce_scatter | solution.py:61
  244.6 36.7 %all-reduce.5.cloned.1.call-done = f32[256,128]{0,1:T(8,128)} async-done(((f32[256,128]{0,1:T(8,128)}), f32[256,128]{0,1:T(8,128)}) %all-reduce.5.cloned.1.call-update) | async-done | bytes 131088 | tf_op jit(solution)/shard_map/psum | solution.py:61
  282.6 11.8 %psum.39 = f32[3,128]{1,0:T(4,128)S(1)} all-reduce(f32[3,128]{1,0:T(4,128)S(1)} %pad_maximum_fusion.2), channel_id=1, replica_groups=mesh['sub'=8,'rep'=4] {'sub'}, use_global_device_ids=true, to_apply=%region_17.18 | all-reduce | flops 384 | bytes 3072 | tf_op jit(solution)/shard_map/psum | solution.py:80
  (94 shorter events, 19.9 us)
Async XLA Ops:
  6.5 22.9 %copy-start = (bf16[256,512]{1,0:T(8,128)(2,1)S(1)}, bf16[256,512]{1,0:T(8,128)(2,1)}, u32[]{:S(2)}) copy-start(bf16[256,512]{1,0:T(8,128)(2,1)} %param.14) | copy-start | bytes 786436
  6.5 102.4 %reduce-scatter.3.cloned.1.call-start = ((), (), s32[]{:S(2)}) async-start(), calls=%async_computation.2 | async-start | bytes 1179648 | tf_op jit(solution)/shard_map/reduce_scatter | solution.py:61
  7.6 21.8 %copy-start.1 = (f32[256,128]{0,1:T(8,128)}, f32[256,128]{0,1:T(8,128)S(1)}, u32[]{:S(2)}) copy-start(f32[256,128]{0,1:T(8,128)S(1)} %copy.17) | copy-start | bytes 393220
  23.7 123.0 %copy-start.15 = (f32[128]{0:T(128)}, f32[128]{0:T(128)S(1)}, u32[]{:S(2)}) copy-start(f32[128]{0:T(128)S(1)} %sqrt.16) | copy-start | bytes 1540
  23.8 3.6 %collective-permute-start.1 = (bf16[256,128]{0,1:T(8,128)(2,1)S(1)}, bf16[256,128]{0,1:T(8,128)(2,1)S(1)}, u32[]{:S(2)}, u32[]{:S(2)}) collective-permute-start(bf16[256,128]{0,1:T(8,128)(2,1)S(1)} %fusion.79), channel_id=1, source_target_pairs={{4,0},{8,4},{12,8},{16,12},{20,16},{24,20},{28,24},{0,28},{5,1},{9... | collective-permute-start | bytes 196616 | tf_op jit(solution)/shard_map/ppermute | solution.py:19
  23.9 4.6 %collective-permute-start = (bf16[256,128]{0,1:T(8,128)(2,1)S(1)}, bf16[256,128]{0,1:T(8,128)(2,1)S(1)}, u32[]{:S(2)}, u32[]{:S(2)}) collective-permute-start(bf16[256,128]{0,1:T(8,128)(2,1)S(1)} %fusion.79), channel_id=1, source_target_pairs={{0,4},{4,8},{8,12},{12,16},{16,20},{20,24},{24,28},{28,0},{1,5},{5... | collective-permute-start | bytes 196616 | tf_op jit(solution)/shard_map/ppermute | solution.py:17
  56.6 89.0 %copy-start.9 = (f32[256,128]{0,1:T(8,128)S(1)}, f32[256,128]{0,1:T(8,128)}, u32[]{:S(2)}) copy-start(f32[256,128]{0,1:T(8,128)} %get-tuple-element.149) | copy-start | bytes 393220
  56.6 89.0 %copy-start.11 = (bf16[256,256]{1,0:T(8,128)(2,1)S(1)}, bf16[256,256]{1,0:T(8,128)(2,1)}, u32[]{:S(2)}) copy-start(bf16[256,256]{1,0:T(8,128)(2,1)} %param.13) | copy-start | bytes 393220
  56.7 89.0 %copy-start.14 = (bf16[256,128]{0,1:T(8,128)(2,1)S(1)}, bf16[256,128]{0,1:T(8,128)(2,1)}, u32[]{:S(2)}) copy-start(bf16[256,128]{0,1:T(8,128)(2,1)} %copy-done.13) | copy-start | bytes 196612
  56.7 90.1 %copy-start.2 = (f32[256,128]{0,1:T(8,128)S(1)}, f32[256,128]{0,1:T(8,128)}, u32[]{:S(2)}) copy-start(f32[256,128]{0,1:T(8,128)} %copy-done.1) | copy-start | bytes 393220
  59.3 86.3 %all-reduce.3.cloned.1.call-start = ((), (), s32[]{:S(2)}) async-start(), calls=%async_computation.3 | async-start | bytes 262144 | tf_op jit(solution)/shard_map/psum | solution.py:61
  109.0 135.6 %reduce-scatter.5.cloned.1.call-start = ((), (), s32[]{:S(2)}) async-start(), calls=%async_computation.4 | async-start | bytes 1179648 | tf_op jit(solution)/shard_map/reduce_scatter | solution.py:61
  160.1 7.1 %copy-start.3 = (f32[256,128]{0,1:T(8,128)}, f32[256,128]{0,1:T(8,128)S(1)}, u32[]{:S(2)}) copy-start(f32[256,128]{0,1:T(8,128)S(1)} %get-tuple-element.144) | copy-start | bytes 393220
  160.2 2.0 collective-permute-start.3
  160.3 5.3 %collective-permute-start.2 = (bf16[256,128]{0,1:T(8,128)(2,1)S(1)}, bf16[256,128]{0,1:T(8,128)(2,1)S(1)}, u32[]{:S(2)}, u32[]{:S(2)}) collective-permute-start(bf16[256,128]{0,1:T(8,128)(2,1)S(1)} %get-tuple-element.143), channel_id=1, source_target_pairs={{0,4},{4,8},{8,12},{12,16},{16,20},{20,24},{24,28},{28,0},{1,5},{5... | collective-permute-start | bytes 196616 | tf_op jit(solution)/shard_map/ppermute | solution.py:17
  193.9 87.4 %copy-start.5 = (f32[256,128]{0,1:T(8,128)S(1)}, f32[256,128]{0,1:T(8,128)}, u32[]{:S(2)}) copy-start(f32[256,128]{0,1:T(8,128)} %get-tuple-element.151) | copy-start | bytes 393220
  193.9 87.4 %copy-start.7 = (bf16[256,128]{0,1:T(8,128)(2,1)S(1)}, bf16[256,128]{0,1:T(8,128)(2,1)}, u32[]{:S(2)}) copy-start(bf16[256,128]{0,1:T(8,128)(2,1)} %copy-done.6) | copy-start | bytes 196612
  193.9 87.4 %copy-start.12 = (bf16[256,256]{1,0:T(8,128)(2,1)S(1)}, bf16[256,256]{1,0:T(8,128)(2,1)}, u32[]{:S(2)}) copy-start(bf16[256,256]{1,0:T(8,128)(2,1)} %param.13) | copy-start | bytes 393220
  193.9 88.6 %copy-start.4 = (f32[256,128]{0,1:T(8,128)S(1)}, f32[256,128]{0,1:T(8,128)}, u32[]{:S(2)}) copy-start(f32[256,128]{0,1:T(8,128)} %copy-done.3) | copy-start | bytes 393220
  194.0 88.6 %copy-start.8 = (f32[1,256,128]{1,2,0:T(8,128)S(1)}, f32[1,256,128]{1,2,0:T(8,128)}, u32[]{:S(2)}) copy-start(f32[1,256,128]{1,2,0:T(8,128)} %get-tuple-element.145) | copy-start | bytes 393220
  194.0 100.5 %copy-start.17 = (f32[128]{0:T(128)S(1)}, f32[128]{0:T(128)}, u32[]{:S(2)}) copy-start(f32[128]{0:T(128)} %copy-done.16) | copy-start | bytes 1540
  194.0 100.5 %copy-start.19 = (f32[128]{0:T(128)S(1)}, f32[128]{0:T(128)}, u32[]{:S(2)}) copy-start(f32[128]{0:T(128)} %copy-done.18) | copy-start | bytes 1540
  194.0 100.5 %copy-start.10 = (f32[256,128]{0,1:T(8,128)S(1)}, f32[256,128]{0,1:T(8,128)}, u32[]{:S(2)}) copy-start(f32[256,128]{0,1:T(8,128)} %get-tuple-element.149) | copy-start | bytes 393220
  196.7 84.6 %all-reduce.5.cloned.1.call-start = ((), (), s32[]{:S(2)}) async-start(), calls=%async_computation.5 | async-start | bytes 262144 | tf_op jit(solution)/shard_map/psum | solution.py:61
  (5 other events, 10.7 us)
Sparse Core Ops, SparseCore 0:
  59.5 49.4 reduce-scatter.2
  111.3 34.3 all-reduce.2
  196.8 47.6 reduce-scatter.4
  246.8 34.4 all-reduce.4
where the time goes:
time: 303 us; the launch traced here: 302 us
  waiting for transfers between devices  177 us (58%)
  blocking collectives  58.8 us (19%)
  local copies, waits for them, and re-layouts  20.7 us (7%)
  matrix products  19.1 us (6%)
  between operations  13.5 us (4%)
  other arithmetic  9.24 us (3%)
    reduce_scatter x2, waiting for transfers between devices, apply_schur(): lax.psum_scatter(lax.psum(flat, 'rep'), 'sub', scatter_dimension=0, tiled...  97.3 us
    psum x2, waiting for transfers between devices, apply_schur(): lax.psum(flat, 'rep')  73.4 us
    psum x2, blocking collectives, orthogonal(): totals = lax.psum(local_sums, 'sub')  23.6 us
    all_gather x2, blocking collectives, apply_schur(): whole = lax.all_gather(rounded, 'sub', axis=0, tiled=True)  20.1 us
    psum x1, blocking collectives, on_device(): start_norm = jnp.sqrt(lax.psum(column_sums(rhs, rhs), 'sub'))  15.1 us
    dot_general x2, matrix products, slot_step(): jnp.dot(factor, first, preferred_element_type=jnp.float32)  7.62 us
    dot_general x2, matrix products, slot_step(): lax.dot_general(coupling, third, transposed, preferred_element_type=jnp.f...  7.46 us
  transfers between devices with their start and end apart: 8, of which 7 were waited for; matrix products, arithmetic and copies ran while one was open for 1% of the time, Pallas kernels for 0%

commit v1 on v0

v1 whole, which is shorter than its diff:
```python
import functools

import jax
import jax.numpy as jnp
from jax import lax
from jax.experimental import pallas as pl
from jax.experimental.pallas import tpu as pltpu
from jax.sharding import PartitionSpec as P

MESH = pl.DeviceIdType.MESH
F32 = jnp.float32
BF16 = jnp.bfloat16
TILE = 512


def kernel(
    n_sub,
    n_rep,
    halo_ids_hbm,
    block_ids_hbm,
    counts,
    rhs_hbm,
    schur_diag_hbm,
    precond_hbm,
    factors_hbm,
    couplings_hbm,
    out,
    halo_ids,
    block_ids,
    rhs,
    schur_diag,
    precond,
    factors,
    couplings,
    product,
    operator,
    pieces,
    halo_rhs,
    halo_w,
    dots_plane,
    dots_chain,
    field_all,
    sib_out,
    sib_in,
    mine,
    plane_out,
    plane_in,
    chain_out,
    chain_in,
    w_all,
    w_rounded,
    weight_sem,
    small_sem,
    halo_send,
    halo_recv,
    dots_send,
    dots_recv,
    chain_dots_send,
    chain_dots_recv,
    field_send,
    field_recv,
    pass_send,
    sib_send,
    sib_recv,
    plane_send,
    plane_recv,
    chain_send,
    chain_recv,
    w_send,
    w_recv,
):
    me = lax.axis_index("sub")
    layer = lax.axis_index("rep")
    core = lax.rem(me, 2)
    chip = me // 2
    sibling = me + 1 - 2 * core
    n_chip = n_sub // 2
    slots, order, width = couplings.shape
    per_slot = block_ids.shape[1]
    rows, columns = rhs.shape
    block = width // per_slot
    owned = rows // block
    share = rows // n_rep
    halo = halo_ids.shape[1]
    started = []

    def send(src, dst, send_sem, recv_sem, device):
        copy = pltpu.make_async_remote_copy(
            src_ref=src,
            dst_ref=dst,
            send_sem=send_sem,
            recv_sem=recv_sem,
            device_id=device,
            device_id_type=MESH,
        )
        copy.start()
        started.append(copy)

    def arrived(dst, send_sem, recv_sem, device):
        pltpu.make_async_remote_copy(
            src_ref=dst,
            dst_ref=dst,
            send_sem=send_sem,
            recv_sem=recv_sem,
            device_id=device,
            device_id_type=MESH,
        ).wait_recv()

    def sub_at(step):
        return lax.rem(me + step, n_sub)

    def layer_at(step):
        return lax.rem(layer + step, n_rep)

    small = [
        pltpu.make_async_copy(src, dst, small_sem.at[place])
        for place, (src, dst) in enumerate(
            (
                (rhs_hbm, rhs),
                (halo_ids_hbm, halo_ids),
                (block_ids_hbm, block_ids),
                (precond_hbm, precond),
                (schur_diag_hbm, schur_diag),
            )
        )
    ]
    for load in small:
        load.start()
    loads = []
    for slot in range(slots):
        loads.append(
            (
                pltpu.make_async_copy(
                    couplings_hbm.at[slot], couplings.at[slot], weight_sem.at[slot, 0]
                ),
                pltpu.make_async_copy(
                    factors_hbm.at[slot], factors.at[slot], weight_sem.at[slot, 1]
                ),
            )
        )
        for load in loads[slot]:
            load.start()

    barrier = pltpu.get_barrier_semaphore()
    for step in range(1, n_sub):
        pl.semaphore_signal(barrier, inc=1, device_id={"sub": sub_at(step)}, device_id_type=MESH)
    for step in range(1, n_rep):
        pl.semaphore_signal(barrier, inc=1, device_id={"rep": layer_at(step)}, device_id_type=MESH)
    pl.semaphore_wait(barrier, n_sub - 1 + n_rep - 1)

    def column_sums(left, right):
        return jnp.sum(left * right, axis=0, keepdims=True)

    def packed(sums):
        pad = jnp.zeros((8 - len(sums), columns), F32)
        return jnp.concatenate(sums + [pad], axis=0)

    def send_dots(stage, value):
        dots_plane[stage, me] = value
        for step in range(1, n_sub):
            send(
                dots_plane.at[stage, me],
                dots_plane.at[stage, me],
                dots_send.at[stage, step],
                dots_recv.at[stage, me],
                {"sub": sub_at(step)},
            )

    def total_dots(stage):
        for step in range(1, n_sub):
            source = sub_at(step)
            arrived(
                dots_plane.at[stage, source],
                dots_send.at[stage, step],
                dots_recv.at[stage, source],
                {"sub": source},
            )
        total = dots_plane[stage, 0]
        for source in range(1, n_sub):
            total = total + dots_plane[stage, source]
        return total

    def send_halo(src, dst, stage):
        send(
            src,
            dst.at[0],
            halo_send.at[stage, 0],
            halo_recv.at[stage, 0],
            {"sub": sub_at(1)},
        )
        send(
            src,
            dst.at[1],
            halo_send.at[stage, 1],
            halo_recv.at[stage, 1],
            {"sub": sub_at(n_sub - 1)},
        )

    def wait_halo(dst, stage):
        for side in range(2):
            arrived(
                dst.at[side],
                halo_send.at[stage, side],
                halo_recv.at[stage, side],
                {"sub": sub_at(n_sub - 1 if side == 0 else 1)},
            )

    def halo_rows(held):
        picked = []
        for j in range(halo):
            side = 0 if j < halo // 2 else 1
            place = lax.rem(halo_ids[0, j], owned)
            blocks = held[side].reshape(owned, block, columns).astype(F32)
            chosen = jnp.zeros((block, columns), F32)
            for b in range(owned):
                chosen = chosen + blocks[b] * jnp.where(place == b, 1.0, 0.0)
            picked.append(chosen)
        return jnp.concatenate(picked, axis=0)

    def build_operator(slot):
        for load in loads[slot]:
            load.wait()
        product[...] = jnp.zeros_like(product)

        def tile_step(tile, carry):
            start = pl.multiple_of(tile * TILE, TILE)
            image = jnp.dot(
                factors[slot, pl.ds(start, TILE), :],
                couplings[slot],
                preferred_element_type=F32,
            ).astype(BF16)
            product[...] += lax.dot_general(
                image, image, (((0,), (0,)), ((), ())), preferred_element_type=F32
            )
            return carry

        lax.fori_loop(0, order // TILE, tile_step, 0)
        leading = product[...].astype(BF16)
        operator[slot, 0] = leading
        operator[slot, 1] = (product[...] - leading.astype(F32)).astype(BF16)

    def precondition(own, halo_part):
        extended = jnp.concatenate([own.astype(BF16), halo_part.astype(BF16)], axis=0)
        return own + jnp.dot(precond[...], extended, preferred_element_type=F32)

    def own_blocks(turn):
        return field_all.at[turn, pl.ds(me * owned, owned)]

    def send_field(turn, field):
        own = own_blocks(turn)
        own[...] = field.astype(BF16).reshape(owned, block, columns)
        for step in range(1, n_chip):
            target = 2 * lax.rem(chip + step, n_chip) + core
            send(
                own,
                own,
                field_send.at[turn, step],
                field_recv.at[turn, me],
                {"sub": target},
            )
        send(
            own,
            own,
            field_send.at[turn, 0],
            field_recv.at[turn, me],
            {"sub": sibling},
        )

    def gather_field(turn):
        for step in range(1, n_chip):
            source = 2 * lax.rem(chip + step, n_chip) + core
            held = field_all.at[turn, pl.ds(source * owned, owned)]
            arrived(held, field_send.at[turn, step], field_recv.at[turn, source], {"sub": source})
            send(
                held,
                held,
                pass_send.at[turn, step],
                field_recv.at[turn, source],
                {"sub": sibling},
            )
        for step in range(n_chip):
            source = 2 * lax.rem(chip + step, n_chip) + 1 - core
            held = field_all.at[turn, pl.ds(source * owned, owned)]
            arrived(held, field_send.at[turn, 0], field_recv.at[turn, source], {"sub": sibling})

    def apply_slots(turn):
        for slot in range(slots):
            picked = jnp.concatenate(
                [field_all[turn, block_ids[slot, j]] for j in range(per_slot)], axis=0
            )
            result = jnp.dot(operator[slot, 0], picked, preferred_element_type=F32) + jnp.dot(
                operator[slot, 1], picked, preferred_element_type=F32
            )
            result = result * jnp.where(counts[0] > slot, 1.0, 0.0)
            pieces[pl.ds(slot * per_slot, per_slot)] = result.reshape(per_slot, block, columns)

    def group_sum(group):
        summed = []
        for b in range(owned):
            total = jnp.zeros((block, columns), F32)
            for slot in range(slots):
                for j in range(per_slot):
                    match = jnp.where(block_ids[slot, j] == group * owned + b, 1.0, 0.0)
                    total = total + pieces[slot * per_slot + j] * match
            summed.append(total)
        return jnp.concatenate(summed, axis=0)

    def reduce_coupled(turn):
        order_of_chips = list(range(1, n_chip)) + [0]
        for step in order_of_chips:
            target = lax.rem(chip + step, n_chip)
            sib_out[turn, step] = group_sum(2 * target + 1 - core).astype(BF16)
            send(
                sib_out.at[turn, step],
                sib_in.at[turn, step],
                sib_send.at[turn, step],
                sib_recv.at[turn, step],
                {"sub": sibling},
            )
        for step in order_of_chips:
            target = lax.rem(chip + step, n_chip)
            mine[step] = group_sum(2 * target + core)
        total = None
        for step in order_of_chips:
            arrived(
                sib_in.at[turn, step],
                sib_send.at[turn, step],
                sib_recv.at[turn, step],
                {"sub": sibling},
            )
            both = mine[step] + sib_in[turn, step].astype(F32)
            if step == 0:
                total = both
            else:
                target = 2 * lax.rem(chip + step, n_chip) + core
                plane_out[turn, step] = both.astype(BF16)
                send(
                    plane_out.at[turn, step],
                    plane_in.at[turn, step],
                    plane_send.at[turn, step],
                    plane_recv.at[turn, step],
                    {"sub": target},
                )
        for step in range(1, n_chip):
            source = 2 * lax.rem(chip + n_chip - step, n_chip) + core
            arrived(
                plane_in.at[turn, step],
                plane_send.at[turn, step],
                plane_recv.at[turn, step],
                {"sub": source},
            )
            total = total + plane_in[turn, step].astype(F32)
        chain_out[turn] = total.reshape(n_rep, share, columns)
        for step in range(1, n_rep):
            target = layer_at(step)
            send(
                chain_out.at[turn, target],
                chain_in.at[turn, step],
                chain_send.at[turn, step],
                chain_recv.at[turn, step],
                {"rep": target},
            )
        result = chain_out[turn, layer]
        for step in range(1, n_rep):
            arrived(
                chain_in.at[turn, step],
                chain_send.at[turn, step],
                chain_recv.at[turn, step],
                {"rep": layer_at(n_rep - step)},
            )
            result = result + chain_in[turn, step]
        return result

    def my_share(ref):
        return ref[pl.ds(pl.multiple_of(layer * share, share), share), :]

    def image_share(turn):
        rounded = own_blocks(turn)[...].reshape(rows, columns)
        local = jnp.dot(my_share(schur_diag), rounded, preferred_element_type=F32)
        return local - reduce_coupled(turn)

    for load in small:
        load.wait()
    send_halo(rhs, halo_rhs, 0)
    send_dots(0, packed([column_sums(rhs[...], rhs[...])]))
    build_operator(0)
    wait_halo(halo_rhs, 0)
    start_norm = jnp.sqrt(total_dots(0)[0:1])
    basis_one = rhs[...] / start_norm
    basis_one_halo = halo_rows(halo_rhs) / start_norm
    dir_one = precondition(basis_one, basis_one_halo)
    out[...] = dir_one
    send_field(0, dir_one)
    for slot in range(1, slots):
        build_operator(slot)
    gather_field(0)
    apply_slots(0)
    w_share = image_share(0) + 3.0 * my_share(out)
    w_all[layer] = w_share
    for step in range(1, n_rep):
        send(
            w_all.at[layer],
            w_all.at[layer],
            w_send.at[step],
            w_recv.at[layer],
            {"rep": layer_at(step)},
        )
    for step in range(1, n_rep):
        source = layer_at(step)
        arrived(w_all.at[source], w_send.at[step], w_recv.at[source], {"rep": source})
    image_one = w_all[...].reshape(rows, columns)
    w_rounded[...] = image_one.astype(BF16)
    send_halo(w_rounded, halo_w, 1)
    send_dots(
        1, packed([column_sums(image_one, basis_one), column_sums(image_one, image_one)])
    )
    sums = total_dots(1)
    upper_one = sums[0:1]
    length_one = jnp.sqrt(sums[1:2] - upper_one * upper_one)
    basis_two = (image_one - upper_one * basis_one) / length_one
    wait_halo(halo_w, 1)
    basis_two_halo = (halo_rows(halo_w) - upper_one * basis_one_halo) / length_one
    dir_two = precondition(basis_two, basis_two_halo)
    send_field(1, dir_two)
    mine[0] = dir_two
    dir_two_share = my_share(mine.at[0])
    mine[0] = basis_two
    basis_two_share = my_share(mine.at[0])
    basis_one_share = my_share(rhs) / start_norm
    gather_field(1)
    apply_slots(1)
    image_two = image_share(1) + 3.0 * dir_two_share
    dots_chain[layer] = packed(
        [
            column_sums(image_two, basis_one_share),
            column_sums(image_two, basis_two_share),
            column_sums(image_two, image_two),
        ]
    )
    for step in range(1, n_rep):
        send(
            dots_chain.at[layer],
            dots_chain.at[layer],
            chain_dots_send.at[step],
            chain_dots_recv.at[layer],
            {"rep": layer_at(step)},
        )
    for step in range(1, n_rep):
        source = layer_at(step)
        arrived(
            dots_chain.at[source],
            chain_dots_send.at[step],
            chain_dots_recv.at[source],
            {"rep": source},
        )
    chain_total = dots_chain[0]
    for source in range(1, n_rep):
        chain_total = chain_total + dots_chain[source]
    send_dots(2, chain_total)
    sums = total_dots(2)
    upper_two = sums[0:1]
    middle = sums[1:2]
    length_two_squared = sums[2:3] - upper_two * upper_two - middle * middle
    radius_one = jnp.sqrt(upper_one * upper_one + length_one * length_one)
    cosine_one = upper_one / radius_one
    sine_one = length_one / radius_one
    rotated_top = cosine_one * upper_two + sine_one * middle
    rotated_low = cosine_one * middle - sine_one * upper_two
    weight_two = (
        -rotated_low * sine_one * start_norm / (rotated_low * rotated_low + length_two_squared)
    )
    weight_one = (cosine_one * start_norm - rotated_top * weight_two) / radius_one
    out[...] = weight_one * out[...] + weight_two * dir_two
    for copy in started:
        copy.wait_send()


def on_device(rhs, schur_diag, precond, halo_ids, factors, couplings, block_ids, counts):
    n_sub = lax.axis_size("sub")
    n_rep = lax.axis_size("rep")
    n_chip = n_sub // 2
    rows, columns = rhs.shape
    slots, order, width = couplings.shape
    per_slot = block_ids.shape[1]
    block = width // per_slot
    owned = rows // block
    share = rows // n_rep
    dma = pltpu.SemaphoreType.DMA
    hbm = pl.BlockSpec(memory_space=pltpu.HBM)
    return pl.pallas_call(
        functools.partial(kernel, n_sub, n_rep),
        out_shape=jax.ShapeDtypeStruct((rows, columns), F32),
        in_specs=[hbm, hbm, pl.BlockSpec(memory_space=pltpu.SMEM)] + [hbm] * 5,
        out_specs=pl.BlockSpec(memory_space=pltpu.VMEM),
        scratch_shapes=[
            pltpu.SMEM(halo_ids.shape, jnp.int32),
            pltpu.SMEM(block_ids.shape, jnp.int32),
            pltpu.VMEM(rhs.shape, F32),
            pltpu.VMEM(schur_diag.shape, BF16),
            pltpu.VMEM(precond.shape, BF16),
            pltpu.VMEM(factors.shape, BF16),
            pltpu.VMEM(couplings.shape, BF16),
            pltpu.VMEM((width, width), F32),
            pltpu.VMEM((slots, 2, width, width), BF16),
            pltpu.VMEM((slots * per_slot, block, columns), F32),
            pltpu.VMEM((2, rows, columns), F32),
            pltpu.VMEM((2, rows, columns), BF16),
            pltpu.VMEM((3, n_sub, 8, columns), F32),
            pltpu.VMEM((n_rep, 8, columns), F32),
            pltpu.VMEM((2, n_sub * owned, block, columns), BF16),
            pltpu.VMEM((2, n_chip, rows, columns), BF16),
            pltpu.VMEM((2, n_chip, rows, columns), BF16),
            pltpu.VMEM((n_chip, rows, columns), F32),
            pltpu.VMEM((2, n_chip, rows, columns), BF16),
            pltpu.VMEM((2, n_chip, rows, columns), BF16),
            pltpu.VMEM((2, n_rep, share, columns), F32),
            pltpu.VMEM((2, n_rep, share, columns), F32),
            pltpu.VMEM((n_rep, share, columns), F32),
            pltpu.VMEM((rows, columns), BF16),
            dma((slots, 2)),
            dma((5,)),
            dma((2, 2)),
            dma((2, 2)),
            dma((3, n_sub)),
            dma((3, n_sub)),
            dma((n_rep,)),
            dma((n_rep,)),
            dma((2, n_chip)),
            dma((2, n_sub)),
            dma((2, n_chip)),
            dma((2, n_chip)),
            dma((2, n_chip)),
            dma((2, n_chip)),
            dma((2, n_chip)),
            dma((2, n_rep)),
            dma((2, n_rep)),
            dma((n_rep,)),
            dma((n_rep,)),
        ],
        compiler_params=pltpu.CompilerParams(
            collective_id=0, has_side_effects=True, vmem_limit_bytes=63 * 1024 * 1024
        ),
        cost_estimate=pl.CostEstimate(
            flops=slots * 2 * order * width * (order + width),
            bytes_accessed=slots * 2 * order * (order + width),
            transcendentals=0,
        ),
    )(halo_ids, block_ids, counts, rhs, schur_diag, precond, factors, couplings)


def solution(mesh):
    placed = (
        P("sub", None),
        P("sub", None),
        P("sub", None),
        P("sub", None),
        P(("sub", "rep"), None, None),
        P(("sub", "rep"), None, None),
        P(("sub", "rep"), None),
        P(("sub", "rep")),
    )
    return jax.shard_map(
        on_device, mesh=mesh, in_specs=placed, out_specs=P("sub", None), check_vma=False
    )
```

time: 303 us -> 65 us (0.21)
  waiting for transfers between devices: 177 us -> 0 us
  Pallas kernels: 0 us -> 62.6 us
  blocking collectives: 58.8 us -> 0 us
  local copies, waits for them, and re-layouts: 20.7 us -> 1.57 us
  matrix products: 19.1 us -> 0 us
  between operations: 13.5 us -> 0.66 us
  other arithmetic: 9.24 us -> 0 us
    reduce_scatter x2 -> x0, waiting for transfers between devices: 97.3 us -> none  [apply_schur(): lax.psum_scatter(lax.psum(flat, 'rep'), 'sub', scatter_dimension=0, tiled...]
    psum x2 -> x0, waiting for transfers between devices: 73.4 us -> none  [apply_schur(): lax.psum(flat, 'rep')]
    pallas_call x0 -> x1, Pallas kernels: none -> 62.6 us  [on_device(): pl.pallas_call(functools.partial(kernel, n_sub, n_rep), out_shape=jax.Sha...]
    psum x3 -> x0, blocking collectives: 38.7 us -> none  [the longest x2 23.6 us: orthogonal(): totals = lax.psum(local_sums, 'sub')]
    all_gather x2 -> x0, blocking collectives: 20.1 us -> none  [apply_schur(): whole = lax.all_gather(rounded, 'sub', axis=0, tiled=True)]
    dot_general x8 -> x0, matrix products: 19.1 us -> none  [the longest x2 7.62 us: slot_step(): jnp.dot(factor, first, preferred_element_type=jnp.float32)]
    ppermute x4 -> x0, waiting for transfers between devices: 5.88 us -> none  [the longest x2 4.43 us: padded_2(): lax.ppermute(tail, axis, [(i, (i + 1) % count) for i in range(count)])]
    reshape x4 -> x0, local copies, waits for them, and re-layouts: 5.56 us -> none  [the longest x2 5.35 us: apply_schur(): flat = total.reshape(-1, columns)]
  transfers between devices with their start and end apart: 8 -> 0, of which waited for: 7 -> 0; matrix products, arithmetic and copies ran while one was open for 1% -> 0% of each run, Pallas kernels for 0% -> 0%
where the time goes in v1:
time: 65 us; the launch traced here: 64.8 us
  Pallas kernels  62.6 us (96%)
  local copies, waits for them, and re-layouts  1.57 us (2%)
  between operations  0.66 us (1%)
    pallas_call x1, Pallas kernels, on_device(): pl.pallas_call(functools.partial(kernel, n_sub, n_rep), out_shape=jax.Sha...  62.6 us
    unnamed x1, local copies, waits for them, and re-layouts  1.57 us

profile of v1, /device:TPU:0, one launch (start us, length us, event | category | flops | bytes accessed | tf_op | source)
XLA Modules:
  0.0 64.8 jit_solution(14786336111655163920)
XLA Ops:
  0.7 62.6 %shard_map.82 = f32[256,128]{1,0:T(8,128)} custom-call(s32[1,2]{1,0:T(1,128)} %halo_ids_hbm.1, s32[2,4]{1,0:T(2,128)} %block_ids_hbm.1, s32[1]{0:T(128)S(6)} %copy.10.counts, f32[256,128]{1,0:T(8,128)} %rhs_hbm.1, bf16[256,256]{1,0:T(8,128)(2,1)} %schur_diag_hbm.1, bf16[256,512]{1,0:T(8,128)(2,1)} %precond_hbm.1, bf16[2,1024,1024]{2,1,0:T(8,128)(2,1)} %factors_hbm.1, ...), custom_call_target="tpu_custom_call" | custom-call | flops 3221225472 | bytes 6291456 | tf_op jit(solution)/shard_map/pallas_call | solution.py:490
  63.3 1.6 %copy.11 = f32[256,128]{1,0:T(8,128)} copy(f32[256,128]{1,0:T(8,128)} %shard_map.82) | data formatting | bytes 262144
